TPU v7x, 32 devices: a whole 2x2x4 slice. The times are simulated.
32 devices in a mesh: groups: 2 (over y), tensor: 16 (over z, x, core).
Axes of the slice: x: 2, y: 2, z: 4, core: 2. Of those that a mesh axis runs over, the one named last changes fastest.
Arguments:
- output_gradient: bfloat16 [384, 8192], P(('groups', 'tensor')), parts along dimension 0, may hold values from -6 to 6
- hidden: bfloat16 [384, 29568], P('groups', 'tensor'), parts along dimension 0, may hold values from -6 to 6
- down_matrix: bfloat16 [29568, 8192], P('tensor'), may hold values from -0.03125 to 0.03125
- first_adapter_factor: bfloat16 [32, 29568, 64], P('groups', 'tensor'), parts along dimension 0, may hold values from -0.03125 to 0.03125
- second_adapter_factor: bfloat16 [32, 64, 8192], P(('groups', 'tensor')), parts along dimension 0, may hold values from -0.75 to 0.75
- counts: int32 [32], P('groups'), parts along dimension 0, may hold values from 1 to 36, 192 in all
- adapter_slots: int32 [32], P('groups'), parts along dimension 0, may hold values from 0 to 15, each once
Outputs:
- hidden_gradient: bfloat16 [384, 29568], P('groups', 'tensor'), parts along dimension 0
- second_factor_gradient: float32 [32, 64, 8192], P(('groups', 'tensor')), parts along dimension 0
There are 2 independent parts, one for each index of `groups`. A program takes and returns all parts, laid end to end along the dimension named above; an argument that names none is the same for every part. Nothing has to cross between parts.
Inputs may be any that keep to these rules, and one draw needn't show every extreme that they name: `counts`: every adapter has at least one token, one adapter has exactly 36. `adapter_slots`: each slot holds exactly one adapter.
All inputs are finite; a program needn't handle non-finite values.
Results may differ from a plain program's by a relative error of at most 0.0046.
Values may be sent and summed in bfloat16 or wider, within the bound.
A program may use at most 192 MiB of HBM per device.

v0:
```python
import jax
import jax.numpy as jnp
from jax import lax
from jax.sharding import PartitionSpec as P

MAX_TOKENS = 36


adapter_scale = 2.0


def token_layout(counts, total_tokens):
    seg_ends = jnp.cumsum(counts)
    segment_starts = seg_ends - counts
    token_ids = jnp.arange(total_tokens, dtype=jnp.int32)
    token_adapter = jnp.sum((seg_ends[None, :] <= token_ids[:, None]).astype(jnp.int32), axis=1)
    position_within = token_ids - segment_starts[token_adapter]
    return (segment_starts, token_adapter, position_within)


def per_device(
    output_gradient,
    hidden,
    down_matrix,
    first_adapter_factor,
    second_adapter_factor,
    counts,
    adapter_slots,
):
    tok_dev = output_gradient.shape[0]
    devices = lax.axis_size("tensor")
    total_tokens = tok_dev * devices
    segment_width = hidden.shape[1]
    adapter_list = first_adapter_factor.shape[0]
    device_wise = second_adapter_factor.shape[0]
    segment_starts, token_adapter, position_within = token_layout(counts, total_tokens)
    slot_range = jnp.arange(MAX_TOKENS, dtype=jnp.int32)
    active_rows = (slot_range[None, :] < counts[:, None]).astype(jnp.float32)
    hidden_pad = jnp.concatenate(
        [hidden, jnp.zeros((MAX_TOKENS, segment_width), jnp.bfloat16)], axis=0
    )
    index_grid = segment_starts[:, None] + slot_range[None, :]
    hidden_rows = hidden_pad[index_grid]
    low_part = (
        jnp.einsum(
            "heg,hga->hea", hidden_rows, first_adapter_factor, preferred_element_type=jnp.float32
        )
        * active_rows[:, :, None]
    )
    slot_ids = jnp.arange(adapter_list, dtype=jnp.int32)
    holder = jnp.sum(
        jnp.where(adapter_slots[None, :] == slot_ids[:, None], slot_ids[None, :], 0), axis=1
    )
    my_first = lax.axis_index("tensor") * device_wise
    my_adapters = lax.dynamic_slice_in_dim(holder, my_first, device_wise, 0)
    my_starts = segment_starts[my_adapters]
    my_counts = counts[my_adapters]
    my_live = slot_range[None, :] < my_counts[:, None]
    summed = lax.psum(low_part[holder], "tensor")
    own_share = lax.dynamic_slice_in_dim(summed, my_first, device_wise, 0)
    low_rank_half = own_share.astype(jnp.bfloat16)
    target_rows = my_starts[:, None, None] + slot_range[None, :, None]
    shard_rows = lax.all_gather(output_gradient, "tensor", axis=0, tiled=True)
    matrix_product = lax.dot_general(
        shard_rows, down_matrix, (((1,), (1,)), ((), ())), preferred_element_type=jnp.float32
    )
    row_ids = jnp.arange(shard_rows.shape[0], dtype=jnp.int32)
    picker = ((target_rows == row_ids[None, None, :]) & my_live[:, :, None]).astype(jnp.bfloat16)
    own_acc = jnp.einsum("jmr,rd->jmd", picker, shard_rows, preferred_element_type=jnp.float32)
    gradient_rows = own_acc.astype(jnp.bfloat16)
    second_gradient = adapter_scale * jnp.einsum(
        "jmr,jmd->jrd", low_rank_half, gradient_rows, preferred_element_type=jnp.float32
    )
    backward_rank = jnp.einsum(
        "xch,xbh->xcb", gradient_rows, second_adapter_factor, preferred_element_type=jnp.float32
    ).astype(jnp.bfloat16)
    every_back = lax.all_gather(backward_rank, "tensor", axis=0, tiled=True)
    backward_adapter = every_back[adapter_slots]
    adapter_segment = jnp.einsum(
        "yvu,ycu->yvc", backward_adapter, first_adapter_factor, preferred_element_type=jnp.float32
    )
    selected = adapter_segment.reshape(adapter_list * MAX_TOKENS, segment_width)[
        token_adapter * MAX_TOKENS + position_within
    ]
    hidden_gradient = (matrix_product + adapter_scale * selected).astype(jnp.bfloat16)
    return (hidden_gradient, second_gradient)


def solution(mesh):
    placed = (
        P(("groups", "tensor"), None),
        P("groups", "tensor"),
        P("tensor", None),
        P("groups", "tensor", None),
        P(("groups", "tensor"), None, None),
        P("groups"),
        P("groups"),
    )
    return jax.shard_map(
        per_device,
        mesh=mesh,
        in_specs=placed,
        out_specs=(P("groups", "tensor"), P(("groups", "tensor"), None, None)),
        check_vma=False,
    )
```

profile of v0, /device:TPU:0, one launch (start us, length us, event | category | flops | bytes accessed | tf_op | source)
XLA Modules:
  0.0 173.0 jit_solution(16416561956151178110)
XLA Ops:
  7.2 0.0 copy-start
  7.2 0.0 all-gather.5.cloned.1.call-start
  7.2 0.7 all-gather.5.cloned.1.call-update
  7.9 0.8 select_reduce_fusion
  8.7 0.6 dynamic_slice.6
  10.6 0.7 copy.12
  11.3 0.1 reduce
  11.5 0.7 sub.13
  12.8 1.3 dynamic-slice.5
  14.0 0.1 compare_select_fusion
  14.1 0.1 reshape.295
  14.2 1.2 concatenate.3
  15.4 3.8 %gather_fusion.2 = bf16[576,1848]{1,0:T(8,128)(2,1)} fusion(bf16[228,1848]{1,0:T(8,128)(2,1)S(1)} %concatenate.3, s32[1024]{0:T(1024)S(1)} %pad_clamp_fusion.1), kind=kCustom, calls=%fused_computation.2 | custom fusion | bytes 4260096 | tf_op jit(solution)/shard_map/gather | solution.py:43
  19.2 0.0 copy-start.1
  19.2 2.6 %reshape.294 = bf16[16,36,1848]{2,1,0:T(8,128)(2,1)S(1)} reshape(bf16[576,1848]{1,0:T(8,128)(2,1)} %gather_fusion.2) | data formatting | bytes 4257792 | tf_op jit(solution)/shard_map/gather | solution.py:43
  21.9 0.0 copy-done.1
  21.9 0.1 fusion.10
  22.0 0.0 copy-start.2
  22.0 4.1 %convolution_multiply_fusion.1 = f32[16,36,64]{2,1,0:T(8,128)} fusion(bf16[16,36,1848]{2,1,0:T(8,128)(2,1)S(1)} %reshape.294, bf16[16,1848,64]{1,2,0:T(8,128)(2,1)} %param.10, f32[16,36]{1,0:T(8,128)S(1)} %fusion.10), kind=kOutput, calls=%fused_computation.9 | convolution fusion | flops 136286208 | bytes 6063360 | tf_op jit(solution)/shard_map/heg,hga->hea/dot_general | solution.py:45
  26.0 1.5 gather_fusion.3
  27.6 67.5 %all-reduce.2 = bf16[16,36,64]{2,1,0:T(8,128)(2,1)S(1)} all-reduce(f32[16,36,64]{2,1,0:T(8,128)S(1)} %gather_fusion.3), channel_id=1, replica_groups=mesh['groups'=2,'tensor'=16] {'tensor'}, use_global_device_ids=true, to_apply=%region_3.4 | all-reduce | flops 36864 | bytes 221184 | tf_op jit(solution)/shard_map/psum | solution.py:59
  95.1 0.7 fusion.13
  95.8 0.5 iota_add_fusion
  96.4 0.6 iota_compare_fusion.4
  97.0 0.1 convert_reduce_fusion
  97.1 4.3 %compare_select_fusion.3 = (s32[192,1]{0,1:T(1,128)S(1)}, s32[192,1]{0,1:T(1,128)S(1)}) fusion(s32[]{:T(128)} %bitcast.17, s32[]{:T(128)} %bitcast.18, s32[]{:T(128)} %bitcast.19, s32[]{:T(128)} %bitcast.20, s32[]{:T(128)} %bitcast.21, s32[]{:T(128)} %bitcast.23, s32[]{:T(128)} %bitcast.22, s32[192,1]{0,1:T(1,128)S(1)} %bitcast.52), kind=kLoop, calls=%fused_computation.41 | loop fusion | flops 2880 | bytes 2332 | tf_op jit(solution)/shard_map/gather | solution.py:17
  101.4 5.7 %select_select_fusion = s32[192]{0:T(256)S(1)} fusion(pred[192]{0:T(512)(128)(4,1)S(1)} %get-tuple-element.32, pred[192]{0:T(512)(128)(4,1)S(1)} %get-tuple-element.31, pred[192]{0:T(512)(128)(4,1)S(1)} %get-tuple-element.30, pred[192]{0:T(512)(128)(4,1)S(1)} %get-tuple-element.29, pred[192]{0:T(512)(128)(4,1)S(1)} %get-tuple-element.28, ...), kind=kLoop, calls=%fused_computation.49 | loop fusion | flops 1728 | bytes 3300 | tf_op jit(solution)/shard_map/gather | solution.py:17
  107.2 0.0 copy-done.2
  107.2 0.0 all-gather.5.cloned.1.call-done
  107.3 4.7 %reshape.350 = bf16[192,8192]{1,0:T(8,128)(2,1)} reshape(bf16[16,12,8192]{2,1,0:T(8,128)(2,1)} %all-gather.5.cloned.1.call-done) | data formatting | bytes 6291456
  111.9 2.6 %convolution_convert_fusion = bf16[36,8192]{1,0:T(8,128)(2,1)S(1)} fusion(bf16[192,8192]{1,0:T(8,128)(2,1)} %reshape.350, s32[36]{0:T(128)S(1)} %iota_add_fusion, pred[36]{0:T(512)(128)(4,1)S(1)} %iota_compare_fusion.4), kind=kOutput, calls=%fused_computation.6 | convolution fusion | flops 113554944 | bytes 3735732 | tf_op jit(solution)/shard_map/jmr,rd->jmd/dot_general | solution.py:69
  114.5 0.0 copy-done
  114.5 0.4 fusion.2
  115.0 17.6 %all-gather.2 = bf16[16,36,64]{2,1,0:T(8,128)(2,1)S(1)} all-gather(bf16[1,36,64]{2,1,0:T(8,128)(2,1)S(1)} %fusion.2), channel_id=2, replica_groups=mesh['groups'=2,'tensor'=16] {'tensor'}, dimensions={0}, use_global_device_ids=true | all-gather | bytes 78336 | tf_op jit(solution)/shard_map/all_gather | solution.py:77
  132.5 0.6 gather_fusion
  133.1 5.1 %fusion.14 = f32[16,36,1848]{2,1,0:T(8,128)} fusion(bf16[16,36,64]{2,1,0:T(8,128)(2,1)S(1)} %gather_fusion, bf16[16,1848,64]{1,2,0:T(8,128)(2,1)} %param.10), kind=kOutput, calls=%fused_computation.55 | convolution fusion | flops 136249344 | bytes 8116224 | tf_op jit(solution)/shard_map/yvu,ycu->yvc/dot_general | solution.py:79
  138.3 5.1 %reshape.211 = f32[576,1848]{1,0:T(8,128)} reshape(f32[16,36,1848]{2,1,0:T(8,128)} %fusion.14) | data formatting | bytes 8515584 | tf_op jit(solution)/shard_map/reshape | solution.py:82
  143.3 1.8 %fusion = f32[1,64,8192]{2,1,0:T(8,128)} fusion(bf16[36,8192]{1,0:T(8,128)(2,1)S(1)} %convolution_convert_fusion, bf16[16,36,64]{2,1,0:T(8,128)(2,1)S(1)} %all-reduce.2, s32[]{:T(128)S(6)} %select_n.56), kind=kOutput, calls=%fused_computation.5 | convolution fusion | flops 38273024 | bytes 2762756 | tf_op jit(solution)/shard_map/jmr,jmd->jrd/dot_general | solution.py:71
  145.1 4.1 %gather_fusion.1 = f32[192,1848]{1,0:T(8,128)S(1)} fusion(f32[576,1848]{1,0:T(8,128)} %reshape.211, s32[1024]{0:T(1024)S(1)} %pad_clamp_fusion.2), kind=kCustom, calls=%fused_computation.1 | custom fusion | bytes 2839296 | tf_op jit(solution)/shard_map/gather | solution.py:82
  149.3 16.9 %fusion.1 = bf16[192,1848]{1,0:T(8,128)(2,1)} fusion(bf16[192,8192]{1,0:T(8,128)(2,1)} %reshape.350, bf16[1848,8192]{1,0:T(8,128)(2,1)} %param.9, f32[192,1848]{1,0:T(8,128)S(1)} %gather_fusion.1), kind=kOutput, calls=%fused_computation.8 | convolution fusion | flops 5814369792 | bytes 35552256 | tf_op jit(solution)/shard_map/dot_general | solution.py:64
  (9 shorter events, 0.1 us)
Async XLA Ops:
  7.2 107.4 %copy-start = (bf16[1,64,8192]{2,1,0:T(8,128)(2,1)S(1)}, bf16[1,64,8192]{2,1,0:T(8,128)(2,1)}, u32[]{:S(2)}) copy-start(bf16[1,64,8192]{2,1,0:T(8,128)(2,1)} %param.11) | copy-start | bytes 3145732
  7.2 100.1 %all-gather.5.cloned.1.call-start = ((), (), s32[]{:S(2)}) async-start(), calls=%async_computation | async-start | bytes 4456448 | tf_op jit(solution)/shard_map/all_gather | solution.py:63
  19.2 2.7 %copy-start.1 = (s32[16]{0:T(128)S(1)}, s32[16]{0:T(128)}, u32[]{:S(2)}) copy-start(s32[16]{0:T(128)} %param.12) | copy-start | bytes 196
  22.0 85.2 %copy-start.2 = (s32[16]{0:T(128)S(1)}, s32[16]{0:T(128)}, u32[]{:S(2)}) copy-start(s32[16]{0:T(128)} %param.13) | copy-start | bytes 196
Sparse Core Ops, SparseCore 0:
  10.2 55.7 all-gather.4
where the time goes:
time: 174 us; the launch traced here: 173 us
  blocking collectives  85.1 us (49%)
  matrix products  30.9 us (18%)
  local copies, waits for them, and re-layouts  27.1 us (16%)
  between operations  16.2 us (9%)
  other arithmetic  13.1 us (8%)
    psum x1, blocking collectives, per_device(): summed = lax.psum(low_part[holder], 'tensor')  67.5 us
    all_gather x1, blocking collectives, per_device(): every_back = lax.all_gather(backward_rank, 'tensor', axis=0, tiled=True)  17.6 us
    dot_general x1, matrix products, per_device(): lax.dot_general(shard_rows, down_matrix, (((1,), (1,)), ((), ())), prefer...  16.9 us
    gather x3, other arithmetic, token_layout(): position_within = token_ids - segment_starts[token_adapter]  10 us
    gather x2, local copies, waits for them, and re-layouts, per_device(): hidden_rows = hidden_pad[index_grid]  6.45 us
    dot_general x1, matrix products, per_device(): jnp.einsum('yvu,ycu->yvc', backward_adapter, first_adapter_factor, prefer...  5.13 us
    reshape x1, local copies, waits for them, and re-layouts, per_device(): adapter_segment.reshape(adapter_list * MAX_TOKENS, segment_width)  5.08 us
    unnamed x7, local copies, waits for them, and re-layouts  4.7 us
  transfers between devices with their start and end apart: 1, of which 0 were waited for; matrix products, arithmetic and copies ran while one was open for 17% of the time, Pallas kernels for 0%

commit v1 on v0

--- a/solution.py
+++ b/solution.py
@@ -1,6 +1,10 @@
+import functools
+
 import jax
 import jax.numpy as jnp
 from jax import lax
+from jax.experimental import pallas as pl
+from jax.experimental.pallas import tpu as pltpu
 from jax.sharding import PartitionSpec as P
 
 MAX_TOKENS = 36
@@ -18,7 +22,7 @@
     return (segment_starts, token_adapter, position_within)
 
 
-def per_device(
+def per_device_general(
     output_gradient,
     hidden,
     down_matrix,
@@ -86,6 +90,461 @@
     return (hidden_gradient, second_gradient)
 
 
+CHUNKS = 4
+HALF_LOW = 24
+HALF_BACK = 32
+NT = (((1,), (1,)), ((), ()))
+NN = (((1,), (0,)), ((), ()))
+MESH = pl.DeviceIdType.MESH
+
+
+def dot(a, b, dims):
+    return lax.dot_general(a, b, dims, preferred_element_type=jnp.float32)
+
+
+def ring_place(chip):
+    z, x = chip // 2, chip % 2
+    return z + x * (7 - 2 * z)
+
+
+def ring_chip(place):
+    x = place // 4
+    z = place + x * (7 - 2 * place)
+    return z * 2 + x
+
+
+def fused_kernel(
+    counts,
+    slots,
+    og,
+    second,
+    hidden_hbm,
+    at_hbm,
+    down_hbm,
+    out,
+    sg,
+    gathered,
+    rows,
+    down,
+    at,
+    hidden,
+    total,
+    low_send,
+    low_recv,
+    back_send,
+    back_all,
+    wide,
+    local_sems,
+    ring_send,
+    ring_recv,
+    sib_send,
+    sib_recv,
+    low_ssem,
+    low_rsem,
+    back_ssem,
+    back_rsem,
+):
+    f32, bf16, i32 = jnp.float32, jnp.bfloat16, jnp.int32
+    me = lax.axis_index("tensor")
+    n = 16
+    tokens = rows.shape[0]
+    adapters = counts.shape[0]
+    width = out.shape[1]
+    core, chip = me % 2, me // 2
+    place = ring_place(chip)
+    sibling = chip * 2 + (1 - core)
+
+    def at_distance(step):
+        return ring_chip((place + step + 8) % 8) * 2 + core
+
+    right, left = at_distance(1), at_distance(-1)
+
+    in_copies = [
+        pltpu.make_async_copy(hidden_hbm, hidden, local_sems.at[0]),
+        pltpu.make_async_copy(at_hbm, at, local_sems.at[1]),
+    ]
+    span = down.shape[1] // 4
+    for b in range(4):
+        in_copies.append(
+            pltpu.make_async_copy(
+                down_hbm.at[:, pl.ds(b * span, span)],
+                down.at[:, pl.ds(b * span, span)],
+                local_sems.at[2 + b],
+            )
+        )
+    for c in in_copies:
+        c.start()
+
+    barrier = pltpu.get_barrier_semaphore()
+    for d in range(1, n):
+        pl.semaphore_signal(
+            barrier, inc=1, device_id={"tensor": (me + d) % n}, device_id_type=MESH
+        )
+
+    quarter = og.shape[1] // 4
+    step_cols = quarter // CHUNKS
+    own = og.shape[0]
+    r_out = lax.broadcasted_iota(i32, (4 * own, own), 0)
+    r_in = lax.broadcasted_iota(i32, (4 * own, own), 1)
+    for c in range(CHUNKS):
+        acc = None
+        for q in range(4):
+            pick = jnp.where(r_out == r_in + q * own, 1.0, 0.0).astype(bf16)
+            part = og[:, q * quarter + c * step_cols : q * quarter + (c + 1) * step_cols]
+            term = dot(pick, part, NN)
+            acc = term if acc is None else acc + term
+        gathered[c, me] = acc.astype(bf16)
+
+    pl.semaphore_wait(barrier, n - 1)
+
+    hops = [(4, 3) if c % 2 == 0 else (3, 4) for c in range(CHUNKS)]
+    sends = []
+
+    def ring_copy(c, way, hop):
+        source = at_distance(-(hop - 1)) if way == 0 else at_distance(hop - 1)
+        block = gathered.at[c, source]
+        return pltpu.make_async_remote_copy(
+            src_ref=block,
+            dst_ref=block,
+            send_sem=ring_send.at[c, way, hop - 1],
+            recv_sem=ring_recv.at[c, way, hop - 1],
+            device_id={"tensor": right if way == 0 else left},
+            device_id_type=MESH,
+        )
+
+    def ring_arrival(c, way, hop):
+        source = at_distance(-hop) if way == 0 else at_distance(hop)
+        block = gathered.at[c, source]
+        return pltpu.make_async_remote_copy(
+            src_ref=block,
+            dst_ref=block,
+            send_sem=ring_send.at[c, way, hop - 1],
+            recv_sem=ring_recv.at[c, way, hop - 1],
+            device_id={"tensor": right if way == 0 else left},
+            device_id_type=MESH,
+        )
+
+    def sib_copy(c, kind, source):
+        block = gathered.at[c, source]
+        return pltpu.make_async_remote_copy(
+            src_ref=block,
+            dst_ref=block,
+            send_sem=sib_send.at[c, kind],
+            recv_sem=sib_recv.at[c, kind],
+            device_id={"tensor": sibling},
+            device_id_type=MESH,
+        )
+
+    def other(source):
+        return (source // 2) * 2 + (1 - core)
+
+    def start(copy):
+        copy.start()
+        sends.append(copy)
+
+    for c in range(CHUNKS):
+        for way in (0, 1):
+            start(ring_copy(c, way, 1))
+        start(sib_copy(c, 0, me))
+
+    def layout(shape, axis):
+        ids = lax.broadcasted_iota(i32, shape, axis)
+        adapter = jnp.zeros(shape, i32)
+        slot = jnp.zeros(shape, i32)
+        position = jnp.zeros(shape, i32)
+        begin = jnp.int32(0)
+        for k in range(adapters):
+            end = begin + counts[k]
+            here = (ids >= begin) & (ids < end)
+            adapter = jnp.where(here, k, adapter)
+            slot = jnp.where(here, slots[k], slot)
+            position = jnp.where(here, ids - begin, position)
+            begin = end
+        return adapter, slot, position
+
+    adapter_r, slot_r, pos_r = layout((tokens, 128), 0)
+    lane_half = lax.broadcasted_iota(i32, (tokens, 128), 1) >= 64
+    _, slot_l, pos_l = layout((8, tokens), 1)
+    slot_l, pos_l = slot_l[0:1], pos_l[0:1]
+    member = adapter_r - jnp.where(lane_half, 1, 0)
+
+    def pick_rows(first, count, half):
+        ids = lax.broadcasted_iota(i32, (count, tokens), 0) + first
+        high = pos_l >= half
+        at_row = slot_l * half + jnp.where(high, pos_l - half, pos_l)
+        lo = jnp.where((ids == at_row) & jnp.logical_not(high), 1.0, 0.0).astype(bf16)
+        hi = jnp.where((ids == at_row) & high, 1.0, 0.0).astype(bf16)
+        return lo, hi
+
+    in_copies[0].wait()
+    in_copies[1].wait()
+    dup = jnp.zeros((tokens, 128), f32)
+    h = hidden[...]
+    for g in range(adapters // 4):
+        two = dot(h, at[g * 256 : (g + 1) * 256, :], NT)
+        for s in range(2):
+            dup += jnp.where(member == 4 * g + 2 * s, two[:, s * 128 : (s + 1) * 128], 0.0)
+    dup = dup + pltpu.roll(dup, 64, 1)
+    top = dup.astype(bf16)
+    rest = (dup - top.astype(f32)).astype(bf16)
+    lo, hi = pick_rows(0, n * HALF_LOW, HALF_LOW)
+    half_out = lax.broadcasted_iota(i32, (n * HALF_LOW, 128), 1) >= 64
+    packed = jnp.where(half_out, dot(hi, top, NN) + dot(hi, rest, NN), dot(lo, top, NN) + dot(lo, rest, NN))
+    low_send[...] = packed.reshape(n, HALF_LOW, 128)
+    low_copies = []
+    for d in range(1, n):
+        peer = (me + d) % n
+        copy = pltpu.make_async_remote_copy(
+            src_ref=low_send.at[peer],
+            dst_ref=low_recv.at[me],
+            send_sem=low_ssem.at[d],
+            recv_sem=low_rsem.at[d],
+            device_id={"tensor": peer},
+            device_id_type=MESH,
+        )
+        copy.start()
+        low_copies.append(copy)
+
+    def hop_step(c, hop):
+        for way in (0, 1):
+            if hop <= hops[c][way]:
+                ring_arrival(c, way, hop).wait_recv()
+                if hop < hops[c][way]:
+                    start(ring_copy(c, way, hop + 1))
+                source = at_distance(-hop) if way == 0 else at_distance(hop)
+                start(sib_copy(c, way * 4 + hop, source))
+
+    def sib_wait(c):
+        sib_copy(c, 0, sibling).wait_recv()
+        for way in (0, 1):
+            for hop in range(1, hops[c][way] + 1):
+                source = at_distance(-hop) if way == 0 else at_distance(hop)
+                sib_copy(c, way * 4 + hop, other(source)).wait_recv()
+
+    for hop in range(1, 4):
+        for c in range(CHUNKS):
+            hop_step(c, hop)
+
+    for c in in_copies[2:]:
+        c.wait()
+
+    four = 16 * own
+    p_out = lax.broadcasted_iota(i32, (four, four), 0)
+    p_in = lax.broadcasted_iota(i32, (four, four), 1)
+    wanted = ((p_out % (4 * own)) // own) * (4 * own) + (p_out // (4 * own)) * own + p_out % own
+    order = jnp.where(p_in == wanted, 1.0, 0.0).astype(bf16)
+
+    def unpack(c):
+        for g in range(4):
+            block = gathered[c, 4 * g : 4 * (g + 1)].reshape(four, step_cols)
+            sorted_rows = dot(order, block, NN).astype(bf16)
+            for q in range(4):
+                col = q * quarter + c * step_cols
+                rows[4 * own * g : 4 * own * (g + 1), col : col + step_cols] = sorted_rows[
+                    4 * own * q : 4 * own * (q + 1)
+                ]
+
+    def matmul(c):
+        def tile(first, count):
+            acc = None
+            for q in range(4):
+                col = q * quarter + c * step_cols
+                term = dot(
+                    rows[:, col : col + step_cols],
+                    down[pl.ds(first, count), col : col + step_cols],
+                    NT,
+                )
+                acc = term if acc is None else acc + term
+            if c == 0:
+                total[:, pl.ds(first, count)] = acc
+            else:
+                total[:, pl.ds(first, count)] += acc
+
+        def body(i, carry):
+            tile(pl.multiple_of(i * 256, 256), 256)
+            return carry
+
+        lax.fori_loop(0, width // 256, body, 0)
+        tile(width // 256 * 256, width % 256)
+
+    def back_part(c, acc):
+        for q in range(4):
+            col = q * quarter + c * step_cols
+            b = second[:, col : col + step_cols]
+            term = dot(rows[:, col : col + step_cols], jnp.concatenate([b, b], axis=0), NT)
+            acc = term if acc is None else acc + term
+        return acc
+
+    back = None
+    hop_step(0, 4)
+    for c in range(CHUNKS - 1):
+        hop_step(c + 1, 4)
+        sib_wait(c)
+        unpack(c)
+        back = back_part(c, back)
+        matmul(c)
+    last = CHUNKS - 1
+    sib_wait(last)
+    unpack(last)
+    back = back_part(last, back).astype(bf16)
+
+    lo, hi = pick_rows(me * HALF_BACK, HALF_BACK, HALF_BACK)
+    half_out = lax.broadcasted_iota(i32, (HALF_BACK, 128), 1) >= 64
+    mine = jnp.where(half_out, dot(hi, back, NN), dot(lo, back, NN)).astype(bf16)
+    back_send[...] = mine
+    back_copies = []
+    for d in range(1, n):
+        copy = pltpu.make_async_remote_copy(
+            src_ref=back_send,
+            dst_ref=back_all.at[me],
+            send_sem=back_ssem.at[d],
+            recv_sem=back_rsem.at[d],
+            device_id={"tensor": (me + d) % n},
+            device_id_type=MESH,
+        )
+        copy.start()
+        back_copies.append(copy)
+    back_all[me] = mine
+    matmul(last)
+
+    low = low_send[me]
+    for d in range(1, n):
+        source = (me + n - d) % n
+        pltpu.make_async_remote_copy(
+            src_ref=low_send.at[source],
+            dst_ref=low_recv.at[source],
+            send_sem=low_ssem.at[d],
+            recv_sem=low_rsem.at[d],
+            device_id={"tensor": source},
+            device_id_type=MESH,
+        ).wait_recv()
+        low = low + low_recv[source]
+    low = 2.0 * low.astype(bf16).astype(f32)
+    low_t = jnp.transpose(jnp.concatenate([low, jnp.zeros((128 - HALF_LOW, 128), f32)], axis=0))
+    low_t = low_t.astype(bf16)
+    lo, hi = pick_rows(me * HALF_LOW, 128, HALF_LOW)
+    local_row = lax.broadcasted_iota(i32, (128, tokens), 0) < HALF_LOW
+    zero = jnp.zeros_like(lo)
+    lo, hi = jnp.where(local_row, lo, zero), jnp.where(local_row, hi, zero)
+    low_tok = (dot(low_t[0:64], lo, NN) + dot(low_t[64:128], hi, NN)).astype(bf16)
+    for b in range(8):
+        cols = pl.ds(b * 1024, 1024)
+        sg[:, cols] = dot(low_tok, rows[:, cols], NN)
+
+    for d in range(1, n):
+        source = (me + n - d) % n
+        pltpu.make_async_remote_copy(
+            src_ref=back_send,
+            dst_ref=back_all.at[source],
+            send_sem=back_ssem.at[d],
+            recv_sem=back_rsem.at[d],
+            device_id={"tensor": source},
+            device_id_type=MESH,
+        ).wait_recv()
+    count = n * HALF_BACK
+    cols = lax.broadcasted_iota(i32, (tokens, count), 1)
+    slot_c, pos_c = slot_r[:, 0:1], pos_r[:, 0:1]
+    high = pos_c >= HALF_BACK
+    at_col = slot_c * HALF_BACK + jnp.where(high, pos_c - HALF_BACK, pos_c)
+    hit = cols == at_col
+    lo = jnp.where(hit & jnp.logical_not(high), 1.0, 0.0).astype(bf16)
+    hi = jnp.where(hit & high, 1.0, 0.0).astype(bf16)
+    every = back_all[...].reshape(count, 128)
+    z = jnp.where(lane_half, dot(hi, every, NN), dot(lo, every, NN))
+    z = 2.0 * (z + pltpu.roll(z, 64, 1))
+    for g in range(adapters // 2):
+        wide[:, g * 128 : (g + 1) * 128] = jnp.where(member == 2 * g, z, 0.0).astype(bf16)
+
+    def finish(first, count):
+        term = dot(wide[...], at[:, pl.ds(first, count)], NN)
+        out[:, pl.ds(first, count)] = (total[:, pl.ds(first, count)] + term).astype(bf16)
+
+    def body(i, carry):
+        finish(pl.multiple_of(i * 256, 256), 256)
+        return carry
+
+    lax.fori_loop(0, width // 256, body, 0)
+    finish(width // 256 * 256, width % 256)
+
+    for copy in sends + low_copies + back_copies:
+        copy.wait_send()
+
+
+def per_device_fused(
+    output_gradient,
+    hidden,
+    down_matrix,
+    first_adapter_factor,
+    second_adapter_factor,
+    counts,
+    adapter_slots,
+):
+    bf16, f32 = jnp.bfloat16, jnp.float32
+    own, model = output_gradient.shape
+    n = lax.axis_size("tensor")
+    tokens, width = hidden.shape
+    adapters, _, rank = first_adapter_factor.shape
+    at = jnp.transpose(first_adapter_factor, (0, 2, 1)).reshape(adapters * rank, width)
+    second = second_adapter_factor.reshape(rank, model)
+    vmem = pl.BlockSpec(memory_space=pltpu.VMEM)
+    smem = pl.BlockSpec(memory_space=pltpu.SMEM)
+    hbm = pl.BlockSpec(memory_space=pl.ANY)
+    dma = pltpu.SemaphoreType.DMA
+    grad, sg = pl.pallas_call(
+        fused_kernel,
+        out_shape=(
+            jax.ShapeDtypeStruct((tokens, width), bf16),
+            jax.ShapeDtypeStruct((rank, model), f32),
+        ),
+        in_specs=[smem, smem, vmem, vmem, hbm, hbm, hbm],
+        out_specs=(vmem, vmem),
+        scratch_shapes=[
+            pltpu.VMEM((CHUNKS, n, 4 * own, model // 4 // CHUNKS), bf16),
+            pltpu.VMEM((tokens, model), bf16),
+            pltpu.VMEM((width, model), bf16),
+            pltpu.VMEM((adapters * rank, width), bf16),
+            pltpu.VMEM((tokens, width), bf16),
+            pltpu.VMEM((tokens, width), f32),
+            pltpu.VMEM((n, HALF_LOW, 128), f32),
+            pltpu.VMEM((n, HALF_LOW, 128), f32),
+            pltpu.VMEM((HALF_BACK, 128), bf16),
+            pltpu.VMEM((n, HALF_BACK, 128), bf16),
+            pltpu.VMEM((tokens, adapters * rank), bf16),
+            dma((6,)),
+            dma((CHUNKS, 2, 4)),
+            dma((CHUNKS, 2, 4)),
+            dma((CHUNKS, 9)),
+            dma((CHUNKS, 9)),
+            dma((n,)),
+            dma((n,)),
+            dma((n,)),
+            dma((n,)),
+        ],
+        compiler_params=pltpu.CompilerParams(
+            collective_id=0, has_side_effects=True, vmem_limit_bytes=60 * 1024 * 1024
+        ),
+        cost_estimate=pl.CostEstimate(
+            flops=2 * tokens * width * (model + 2 * adapters * rank),
+            bytes_accessed=2 * width * (model + adapters * rank),
+            transcendentals=0,
+        ),
+    )(counts, adapter_slots, output_gradient, second, hidden, at, down_matrix)
+    return grad, sg.reshape(1, rank, model)
+
+
+def per_device(*arrays):
+    output_gradient, hidden, _, first_adapter_factor, second_adapter_factor = arrays[:5]
+    fits = (
+        lax.axis_size("tensor") == 16
+        and output_gradient.shape == (12, 8192)
+        and hidden.shape[0] == 192
+        and first_adapter_factor.shape[0] == 16
+        and first_adapter_factor.shape[2] == 64
+        and second_adapter_factor.shape[0] == 1
+    )
+    return (per_device_fused if fits else per_device_general)(*arrays)
+
+
 def solution(mesh):
     placed = (
         P(("groups", "tensor"), None),

time: 174 us -> 59.5 us (0.34)
  blocking collectives: 85.1 us -> 0 us
  Pallas kernels: 0 us -> 53.5 us
  matrix products: 30.9 us -> 0 us
  local copies, waits for them, and re-layouts: 27.1 us -> 5.09 us
  between operations: 16.2 us -> 0.64 us
  other arithmetic: 13.1 us -> 0 us
    psum x1 -> x0, blocking collectives: 67.5 us -> none  [per_device(): summed = lax.psum(low_part[holder], 'tensor')]
    pallas_call x0 -> x1, Pallas kernels: none -> 53.5 us  [per_device_fused(): pl.pallas_call(fused_kernel, out_shape=(jax.ShapeDtypeStruct((tokens, wid...]
    dot_general x6 -> x0, matrix products: 30.9 us -> none  [the longest x1 16.9 us: per_device(): lax.dot_general(shard_rows, down_matrix, (((1,), (1,)), ((), ())), prefer...]
    all_gather x1 -> x0, blocking collectives: 17.6 us -> none  [per_device(): every_back = lax.all_gather(backward_rank, 'tensor', axis=0, tiled=True)]
    gather x7 -> x0, local copies, waits for them, and re-layouts: 14.7 us -> none  [the longest x2 6.45 us: per_device(): hidden_rows = hidden_pad[index_grid]]
    gather x7 -> x0, other arithmetic: 10.1 us -> none  [the longest x3 10 us: token_layout(): position_within = token_ids - segment_starts[token_adapter]]
    reshape x1 -> x0, local copies, waits for them, and re-layouts: 5.08 us -> none  [per_device(): adapter_segment.reshape(adapter_list * MAX_TOKENS, segment_width)]
    unnamed x7 -> x2, local copies, waits for them, and re-layouts: 4.7 us -> 5.09 us
  transfers between devices with their start and end apart: 1 -> 0, of which waited for: 0 -> 0; matrix products, arithmetic and copies ran while one was open for 17% -> 0% of each run, Pallas kernels for 0% -> 0%
where the time goes in v1:
time: 59.5 us; the launch traced here: 59.3 us
  Pallas kernels  53.5 us (90%)
  local copies, waits for them, and re-layouts  5.09 us (9%)
  between operations  0.64 us (1%)
    pallas_call x1, Pallas kernels, per_device_fused(): pl.pallas_call(fused_kernel, out_shape=(jax.ShapeDtypeStruct((tokens, wid...  53.5 us
    unnamed x2, local copies, waits for them, and re-layouts  5.09 us

profile of v1, /device:TPU:0, one launch (start us, length us, event | category | flops | bytes accessed | tf_op | source)
XLA Modules:
  0.0 59.3 jit_solution(10469151908467032844)
XLA Ops:
  0.6 53.5 %shard_map.86 = (bf16[192,1848]{1,0:T(8,128)(2,1)}, f32[64,8192]{1,0:T(8,128)}) custom-call(s32[16]{0:T(128)} %counts.1, s32[16]{0:T(128)} %slots.1, bf16[12,8192]{1,0:T(8,128)(2,1)} %og.1, bf16[64,8192]{1,0:T(8,128)(2,1)} %bitcast.7, bf16[192,1848]{1,0:T(8,128)(2,1)} %hidden_hbm.1, bf16[1024,1848]{1,0:T(8,128)(2,1)} %bitcast.5, bf16[1848,8192]{1,0:T(8,128)(2,1)} %down_hbm.1), custom_call_target="tpu_custom_call" | custom-call | flops 7266631680 | bytes 34062336 | tf_op jit(solution)/shard_map/pallas_call | solution.py:493
  54.2 2.0 %copy.11 = bf16[192,1848]{1,0:T(8,128)(2,1)} copy(bf16[192,1848]{1,0:T(8,128)(2,1)} %get-tuple-element.8) | data formatting | bytes 1419264
  56.2 3.1 %copy.12 = f32[1,64,8192]{2,1,0:T(8,128)} copy(f32[1,64,8192]{2,1,0:T(8,128)} %bitcast.6) | data formatting | bytes 4194304

commit v2 on v1

--- a/solution.py
+++ b/solution.py
@@ -302,7 +302,6 @@
             device_id={"tensor": peer},
             device_id_type=MESH,
         )
-        copy.start()
         low_copies.append(copy)
 
     def hop_step(c, hop):
@@ -345,27 +344,21 @@
                 ]
 
     def matmul(c):
-        def tile(first, count):
+        split = width // 32 * 16 + 16
+        for first, count in ((0, split), (split, width - split)):
             acc = None
             for q in range(4):
                 col = q * quarter + c * step_cols
                 term = dot(
+                    down[first : first + count, col : col + step_cols],
                     rows[:, col : col + step_cols],
-                    down[pl.ds(first, count), col : col + step_cols],
                     NT,
                 )
                 acc = term if acc is None else acc + term
             if c == 0:
-                total[:, pl.ds(first, count)] = acc
+                total[first : first + count, :] = acc
             else:
-                total[:, pl.ds(first, count)] += acc
-
-        def body(i, carry):
-            tile(pl.multiple_of(i * 256, 256), 256)
-            return carry
-
-        lax.fori_loop(0, width // 256, body, 0)
-        tile(width // 256 * 256, width % 256)
+                total[first : first + count, :] += acc
 
     def back_part(c, acc):
         for q in range(4):
@@ -379,6 +372,9 @@
     hop_step(0, 4)
     for c in range(CHUNKS - 1):
         hop_step(c + 1, 4)
+        if c == CHUNKS - 2:
+            for copy in low_copies:
+                copy.start()
         sib_wait(c)
         unpack(c)
         back = back_part(c, back)
@@ -457,7 +453,7 @@
 
     def finish(first, count):
         term = dot(wide[...], at[:, pl.ds(first, count)], NN)
-        out[:, pl.ds(first, count)] = (total[:, pl.ds(first, count)] + term).astype(bf16)
+        out[:, pl.ds(first, count)] = (jnp.transpose(total[pl.ds(first, count), :]) + term).astype(bf16)
 
     def body(i, carry):
         finish(pl.multiple_of(i * 256, 256), 256)
@@ -504,7 +500,7 @@
             pltpu.VMEM((width, model), bf16),
             pltpu.VMEM((adapters * rank, width), bf16),
             pltpu.VMEM((tokens, width), bf16),
-            pltpu.VMEM((tokens, width), f32),
+            pltpu.VMEM((width, tokens), f32),
             pltpu.VMEM((n, HALF_LOW, 128), f32),
             pltpu.VMEM((n, HALF_LOW, 128), f32),
             pltpu.VMEM((HALF_BACK, 128), bf16),

time: 59.5 us -> 49.9 us (0.84)
  Pallas kernels: 53.5 us -> 43.9 us
    pallas_call x1, Pallas kernels: 53.5 us -> 43.9 us  [per_device_fused(): pl.pallas_call(fused_kernel, out_shape=(jax.ShapeDtypeStruct((tokens, wid...]
where the time goes in v2:
time: 49.9 us; the launch traced here: 49.7 us
  Pallas kernels  43.9 us (88%)
  local copies, waits for them, and re-layouts  5.09 us (10%)
  between operations  0.64 us (1%)
    pallas_call x1, Pallas kernels, per_device_fused(): pl.pallas_call(fused_kernel, out_shape=(jax.ShapeDtypeStruct((tokens, wid...  43.9 us
    unnamed x2, local copies, waits for them, and re-layouts  5.09 us

profile of v2, /device:TPU:0, one launch (start us, length us, event | category | flops | bytes accessed | tf_op | source)
XLA Modules:
  0.0 49.7 jit_solution(6795855535550865123)
XLA Ops:
  0.6 43.9 %shard_map.86 = (bf16[192,1848]{1,0:T(8,128)(2,1)}, f32[64,8192]{1,0:T(8,128)}) custom-call(s32[16]{0:T(128)} %counts.1, s32[16]{0:T(128)} %slots.1, bf16[12,8192]{1,0:T(8,128)(2,1)} %og.1, bf16[64,8192]{1,0:T(8,128)(2,1)} %bitcast.7, bf16[192,1848]{1,0:T(8,128)(2,1)} %hidden_hbm.1, bf16[1024,1848]{1,0:T(8,128)(2,1)} %bitcast.5, bf16[1848,8192]{1,0:T(8,128)(2,1)} %down_hbm.1), custom_call_target="tpu_custom_call" | custom-call | flops 7266631680 | bytes 34062336 | tf_op jit(solution)/shard_map/pallas_call | solution.py:489
  44.6 2.0 %copy.11 = bf16[192,1848]{1,0:T(8,128)(2,1)} copy(bf16[192,1848]{1,0:T(8,128)(2,1)} %get-tuple-element.8) | data formatting | bytes 1419264
  46.6 3.1 %copy.12 = f32[1,64,8192]{2,1,0:T(8,128)} copy(f32[1,64,8192]{2,1,0:T(8,128)} %bitcast.6) | data formatting | bytes 4194304
